TPU v7x, 256 devices: a whole 4x4x8 slice. The times are simulated.
256 devices in a mesh: keys: 64 (over y, z, core), seq: 4 (over x).
Axes of the slice: x: 4, y: 4, z: 8, core: 2. Of those that a mesh axis runs over, the one named last changes fastest.
Arguments:
- span_queries: bfloat16 [1536, 768], P(('keys', 'seq')), may hold values from -6 to 6
- key_slab: bfloat16 [4096, 768], P('keys'), may hold values from -0.21875 to 0.21875
- neighbour_store: bfloat16 [4096, 64, 896], P('keys'), may hold values from -6 to 6
- neighbour_ids: int32 [1536, 2], P(('keys', 'seq')), may hold values from 0 to 4094, as said below
- attn_queries: bfloat16 [98304, 2048], P(('keys', 'seq')), may hold values from -200 to 200
- kv_weight: bfloat16 [2, 2048, 896], P(None, 'keys'), may hold values from -0.1875 to 0.1875
Outputs:
- best_scores: float32 [1536, 2], P(('keys', 'seq'))
- attended: bfloat16 [98304, 2048], P(('keys', 'seq'))
Inputs may be any that keep to these rules, and one draw needn't show every extreme that they name: `neighbour_ids`: each id c has c mod 64 at most 62, so c + 1 lies on the same shard c // 64. Among the 12 ids of one device's spans (aligned blocks of 6 rows), no shard holds more than 1, and some shard holds exactly 1.
All inputs are finite; a program needn't handle non-finite values.
Results may differ from a plain program's by a relative error of at most 0.012.
The roundings to bfloat16 on the way count: a program that leaves them out, or rounds other values in their place, can miss the bound.
Values may be sent and summed in bfloat16 or wider, within the bound.
A program may use at most 128 MiB of HBM per device.

v0:
```python
import jax
import jax.numpy as jnp
from jax import lax
from jax.sharding import PartitionSpec as P

HEADS = 16
HEAD_DIM = 128


def merged(part, axis, combine):
    gathered = jax.tree.map(lambda a: lax.all_gather(a, axis), part)

    def take(source):
        return jax.tree.map(lambda a: lax.dynamic_index_in_dim(a, source, 0, False), gathered)

    return lax.fori_loop(
        1, lax.axis_size(axis), lambda source, state: combine(state, take(source)), take(0)
    )


def keep_two(left, right):
    higher = jnp.maximum(left[0], right[0])
    runner = jnp.maximum(jnp.minimum(left[0], right[0]), jnp.maximum(left[1], right[1]))
    return (higher, runner)


def best_two(values):
    padding = jnp.full((values.shape[0], 2), -jnp.inf, values.dtype)
    return lax.top_k(jnp.concatenate([values, padding], axis=1), 2)[0]


def row_scores(left, right):
    return lax.dot_general(
        left, right, (((1,), (1,)), ((), ())), preferred_element_type=jnp.float32
    )


def body(span_queries, key_slab, neighbour_store, neighbour_ids, attn_queries, kv_weight):
    key_count = lax.axis_size("keys")
    position = lax.axis_index("keys")
    own_spans = neighbour_ids.shape[0]
    shard_spans = neighbour_store.shape[0]
    span_rows = neighbour_store.shape[1]
    enc_width = neighbour_store.shape[2]
    candidates = best_two(
        row_scores(lax.all_gather(span_queries, "keys", axis=0, tiled=True), key_slab)
    )
    higher_all, runner_all = merged((candidates[:, 0], candidates[:, 1]), "keys", keep_two)
    higher = lax.dynamic_slice_in_dim(higher_all, position * own_spans, own_spans)
    runner = lax.dynamic_slice_in_dim(runner_all, position * own_spans, own_spans)
    best_scores = jnp.stack([higher, runner], axis=1)
    flat_ids = neighbour_ids.reshape(-1)
    need_count = flat_ids.shape[0]
    per_shard = (need_count + key_count - 1) // key_count
    capacity = 2 * per_shard
    target = flat_ids // shard_spans
    offset = flat_ids % shard_spans
    order_index = jnp.arange(need_count, dtype=jnp.int32)
    same_shard = (target[:, None] == target[None, :]) & (
        order_index[:, None] < order_index[None, :]
    )
    slot_base = 2 * jnp.sum(same_shard.astype(jnp.int32), axis=0)
    slot_index = jnp.arange(capacity, dtype=jnp.int32)
    shard_onehot = (target[:, None] == jnp.arange(key_count, dtype=jnp.int32)[None, :]).astype(
        jnp.int32
    )
    first_slot = (slot_index == slot_base[..., None]).astype(jnp.int32) * offset[..., None]
    next_slot = (slot_index == slot_base[..., None] + 1).astype(jnp.int32) * (offset[..., None] + 1)
    table = jnp.einsum("nj,ns->js", shard_onehot, first_slot + next_slot)
    incoming = lax.all_to_all(table, "keys", split_axis=0, concat_axis=0, tiled=True)
    outgoing = neighbour_store[incoming]
    arrived = lax.all_to_all(outgoing, "keys", split_axis=0, concat_axis=0, tiled=True)
    arrived = arrived.reshape(key_count * capacity, span_rows, enc_width)
    first_row = target * capacity + slot_base
    picked = arrived[jnp.stack([first_row, first_row + 1], axis=1)]
    neighbours = picked.reshape(own_spans * 4 * span_rows, enc_width)
    keys_values = jnp.einsum(
        "re,tce->rtc",
        neighbours,
        lax.all_gather(kv_weight, "keys", axis=1, tiled=True),
        preferred_element_type=jnp.float32,
    ).astype(jnp.bfloat16)
    key_rows = keys_values[:, 0].reshape(own_spans, 4 * span_rows, HEADS, HEAD_DIM)
    value_rows = keys_values[:, 1].reshape(own_spans, 4 * span_rows, HEADS, HEAD_DIM)
    queries = attn_queries.reshape(own_spans, span_rows, HEADS, HEAD_DIM)
    logits = jnp.einsum(
        "cqhd,ckhd->chqk", queries, key_rows, preferred_element_type=jnp.float32
    ) * HEAD_DIM ** (-0.5)
    largest = jnp.max(logits, axis=-1, keepdims=True)
    expo_terms = jnp.exp(logits - largest)
    weights = (expo_terms / jnp.sum(expo_terms, axis=-1, keepdims=True)).astype(jnp.bfloat16)
    output = jnp.einsum("chqk,ckhd->cqhd", weights, value_rows, preferred_element_type=jnp.float32)
    attended = output.astype(jnp.bfloat16).reshape(own_spans * span_rows, HEADS * HEAD_DIM)
    return (best_scores, attended)


def solution(mesh):
    return jax.shard_map(
        body,
        mesh=mesh,
        in_specs=(
            P(("keys", "seq"), None),
            P("keys", None),
            P("keys", None, None),
            P(("keys", "seq"), None),
            P(("keys", "seq"), None),
            P(None, "keys", None),
        ),
        out_specs=(P(("keys", "seq"), None), P(("keys", "seq"), None)),
        check_vma=False,
    )
```

profile of v0, /device:TPU:1, one launch (start us, length us, event | category | flops | bytes accessed | tf_op | source)
XLA Modules:
  0.0 606.7 jit_solution(17030885371384447195)
XLA Ops:
  7.2 0.8 copy.33
  8.5 22.2 %all_to_all.17 = s32[64,1,2]{2,1,0:T(1,128)S(1)} all-to-all(s32[64,1,2]{2,1,0:T(1,128)S(1)} %bitcast.81), channel_id=1, replica_groups=mesh['keys'=64,'seq'=4] {'keys'}, dimensions={0} | all-to-all | bytes 1024 | tf_op jit(solution)/shard_map/all_to_all | solution.py:70
  31.1 11.9 %gather_fusion = bf16[128,64,896]{2,1,0:T(8,128)(2,1)} fusion(bf16[64,64,896]{2,1,0:T(8,128)(2,1)} %param.10, s32[1024]{0:T(1024)S(1)} %pad_clamp_fusion.1), kind=kCustom, calls=%fused_computation | custom fusion | bytes 29360640 | tf_op jit(solution)/shard_map/gather | solution.py:71
  43.0 6.2 %all-to-all-start.1 = ((bf16[64,2,64,896]{3,2,1,0:T(8,128)(2,1)}), bf16[64,2,64,896]{3,2,1,0:T(8,128)(2,1)}, u32[]{:S(2)}, u32[]{:S(2)}) async-start(bf16[64,2,64,896]{3,2,1,0:T(8,128)(2,1)} %bitcast.73), calls=%async_computation.1 | async-start | bytes 29360128 | tf_op jit(solution)/shard_map/all_to_all | solution.py:72
  49.3 0.7 all-gather.5.cloned.1.call-update
  50.3 1.6 copy.44
  51.8 380.2 %all-gather.2 = bf16[64,6,768]{2,1,0:T(8,128)(2,1)S(1)} all-gather(bf16[1,6,768]{2,1,0:T(8,128)(2,1)S(1)} %bitcast.82), channel_id=1, replica_groups=mesh['keys'=64,'seq'=4] {'keys'}, dimensions={0}, use_global_device_ids=true | all-gather | bytes 599040 | tf_op jit(solution)/shard_map/all_gather | solution.py:46
  432.5 5.0 top_k.8
  437.6 48.6 %all-gather = f32[24576,1]{0,1:T(1,128)S(1)} all-gather(f32[384,1]{0,1:T(1,128)S(1)} %get-tuple-element.161), channel_id=2, replica_groups=mesh['keys'=64,'seq'=4] {'keys'}, dimensions={0}, use_global_device_ids=true | all-gather | bytes 99840 | tf_op jit(solution)/shard_map/all_gather | solution.py:11
  486.7 0.9 reduce.14
  487.6 44.4 %all-gather.1 = f32[24576,1]{0,1:T(1,128)S(1)} all-gather(f32[384,1]{0,1:T(1,128)S(1)} %get-tuple-element.160), channel_id=3, replica_groups=mesh['keys'=64,'seq'=4] {'keys'}, dimensions={0}, use_global_device_ids=true | all-gather | bytes 99840 | tf_op jit(solution)/shard_map/all_gather | solution.py:11
  532.0 0.9 reduce.15
  533.0 4.3 while.17
  537.4 0.6 pad_maximum_fusion
  538.0 6.3 %gather_fusion.1 = bf16[24,64,896]{2,1,0:T(8,128)(2,1)S(1)} fusion(bf16[128,64,896]{2,1,0:T(8,128)(2,1)} %bitcast.6, s32[1024]{0:T(1024)S(1)} %pad_clamp_fusion), kind=kCustom, calls=%fused_computation.1 | custom fusion | bytes 5505120 | tf_op jit(solution)/shard_map/gather | solution.py:75
  544.3 18.7 %convolution_convert_fusion = bf16[1536,2,2048]{2,0,1:T(8,128)(2,1)} fusion(bf16[1536,896,1]{1,0,2:T(8,128)(2,1)S(1)} %bitcast.78, bf16[2,2048,896]{2,1,0:T(8,128)(2,1)} %all-gather.5.cloned.1.call-done), kind=kOutput, calls=%fused_computation.6 | convolution fusion | flops 11280580608 | bytes 22675456 | tf_op jit(solution)/shard_map/re,tce->rtc/dot_general | solution.py:77
  563.0 5.3 slice_bitcast_fusion.1
  568.3 2.3 copy.43
  570.7 3.7 fusion.5
  574.4 2.4 fusion.42
  576.8 5.0 copy.45
  581.8 15.5 %fusion.16 = bf16[6,64,16,128]{3,1,2,0:T(8,128)(2,1)S(1)} fusion(bf16[6,256,16,128]{3,2,1,0:T(8,128)(2,1)} %bitcast.75, f32[6,16,64]{2,1,0:T(8,128)S(1)} %fusion.42, f32[6,16,256,64]{2,3,1,0:T(8,128)} %copy-done.2), kind=kOutput, calls=%fused_computation.24 | convolution fusion | flops 411310336 | bytes 14180352 | tf_op jit(solution)/shard_map/chqk,ckhd->cqhd/dot_general | solution.py:92
  597.3 1.0 copy.42
  598.4 1.6 copy.58
  (166 shorter events, 4.9 us)
Async XLA Ops:
  7.2 425.0 %copy-start = (bf16[64,768]{1,0:T(8,128)(2,1)S(1)}, bf16[64,768]{1,0:T(8,128)(2,1)}, u32[]{:S(2)}) copy-start(bf16[64,768]{1,0:T(8,128)(2,1)} %param.9) | copy-start | bytes 294916
  43.0 7.3 %copy-start.3 = (bf16[384,2048]{1,0:T(8,128)(2,1)S(1)}, bf16[384,2048]{1,0:T(8,128)(2,1)}, u32[]{:S(2)}) copy-start(bf16[384,2048]{1,0:T(8,128)(2,1)} %param.12) | copy-start | bytes 4718596
  43.0 8.8 %copy-start.4 = (bf16[6,768]{1,0:T(8,128)(2,1)S(1)}, bf16[6,768]{1,0:T(8,128)(2,1)}, u32[]{:S(2)}) copy-start(bf16[6,768]{1,0:T(8,128)(2,1)} %param.8) | copy-start | bytes 27652
  43.0 495.0 %all-to-all-start.1 = ((bf16[64,2,64,896]{3,2,1,0:T(8,128)(2,1)}), bf16[64,2,64,896]{3,2,1,0:T(8,128)(2,1)}, u32[]{:S(2)}, u32[]{:S(2)}) async-start(bf16[64,2,64,896]{3,2,1,0:T(8,128)(2,1)} %bitcast.73), calls=%async_computation.1 | async-start | bytes 29360128 | tf_op jit(solution)/shard_map/all_to_all | solution.py:72
  49.2 495.1 %all-gather.5.cloned.1.call-start = ((), (), s32[]{:S(2)}) async-start(), calls=%async_computation.2 | async-start | bytes 7454720 | tf_op jit(solution)/shard_map/all_gather | solution.py:80
  574.4 7.4 %copy-start.2 = (f32[6,16,256,64]{2,3,1,0:T(8,128)}, f32[6,16,256,64]{2,3,1,0:T(8,128)S(1)}, u32[]{:S(2)}) copy-start(f32[6,16,256,64]{2,3,1,0:T(8,128)S(1)} %fusion.5) | copy-start | bytes 18874372
  581.8 18.1 %copy-start.1 = (bf16[64,768]{1,0:T(8,128)(2,1)S(1)}, bf16[64,768]{1,0:T(8,128)(2,1)}, u32[]{:S(2)}) copy-start(bf16[64,768]{1,0:T(8,128)(2,1)} %param.9) | copy-start | bytes 294916
Sparse Core Ops, SparseCore 0:
  52.8 128.8 all-gather.4
where the time goes:
time: 607 us
  blocking collectives  495 us (82%)
  local copies, waits for them, and re-layouts  39 us (6%)
  matrix products  38.6 us (6%)
  between operations  14.2 us (2%)
  other arithmetic  10.8 us (2%)
  starting transfers between devices  6.27 us (1%)
    all_gather x1, blocking collectives, body(): lax.all_gather(span_queries, 'keys', axis=0, tiled=True)  380 us
    all_gather x2, blocking collectives, merged(): gathered = jax.tree.map(lambda a: lax.all_gather(a, axis), part)  93 us
    all_to_all x1, blocking collectives, body(): lax.all_to_all(table, 'keys', split_axis=0, concat_axis=0, tiled=True)  22.2 us
    dot_general x1, matrix products, body(): jnp.einsum('re,tce->rtc', neighbours, lax.all_gather(kv_weight, 'keys', a...  18.7 us
    unnamed x17, local copies, waits for them, and re-layouts  16.8 us
    dot_general x1, matrix products, body(): jnp.einsum('chqk,ckhd->cqhd', weights, value_rows, preferred_element_type...  15.5 us
  transfers between devices with their start and end apart: 2, of which 0 were waited for; matrix products, arithmetic and copies ran while one was open for 3% of the time, Pallas kernels for 0%

commit v1 on v0

--- a/solution.py
+++ b/solution.py
@@ -5,6 +5,28 @@
 
 HEADS = 16
 HEAD_DIM = 128
+
+
+def in_order(tiles, dim):
+    shape = list(tiles.shape[1:])
+    shape[dim] *= tiles.shape[0]
+    return jnp.moveaxis(tiles, 0, dim).reshape(shape)
+
+
+def collected_by_bits(array, axis):
+    size = lax.axis_size(axis)
+    pieces = array[None]
+    for level in range(size.bit_length() - 1):
+        bit = 1 << level
+        other = lax.ppermute(pieces, axis, [(i, i ^ bit) for i in range(size)])
+        both = jnp.stack([pieces, other])
+        upper = lax.axis_index(axis) >> level & 1
+        pieces = jnp.where(upper == 0, both, both[::-1]).reshape(-1, *array.shape)
+    return pieces
+
+
+def gather_by_bits(array, axis, dim):
+    return in_order(collected_by_bits(array, axis), dim)
 
 
 def merged(part, axis, combine):
@@ -42,9 +64,7 @@
     shard_spans = neighbour_store.shape[0]
     span_rows = neighbour_store.shape[1]
     enc_width = neighbour_store.shape[2]
-    candidates = best_two(
-        row_scores(lax.all_gather(span_queries, "keys", axis=0, tiled=True), key_slab)
-    )
+    candidates = best_two(row_scores(gather_by_bits(span_queries, "keys", 0), key_slab))
     higher_all, runner_all = merged((candidates[:, 0], candidates[:, 1]), "keys", keep_two)
     higher = lax.dynamic_slice_in_dim(higher_all, position * own_spans, own_spans)
     runner = lax.dynamic_slice_in_dim(runner_all, position * own_spans, own_spans)

time: 607 us -> 577 us (0.951)
  blocking collectives: 495 us -> 117 us
  waiting for transfers between devices: 0.7 us -> 336 us
  starting transfers between devices: 6.27 us -> 18.8 us
    all_gather x1 -> x0, blocking collectives: 380 us -> none  [body(): lax.all_gather(span_queries, 'keys', axis=0, tiled=True)]
    ppermute x0 -> x6, waiting for transfers between devices: none -> 336 us  [collected_by_bits(): other = lax.ppermute(pieces, axis, [(i, i ^ bit) for i in range(size)])]
    ppermute x0 -> x6, starting transfers between devices: none -> 12.5 us  [collected_by_bits(): other = lax.ppermute(pieces, axis, [(i, i ^ bit) for i in range(size)])]
    unnamed x17 -> x16, local copies, waits for them, and re-layouts: 16.8 us -> 16.6 us
  transfers between devices with their start and end apart: 2 -> 8, of which waited for: 0 -> 6; matrix products, arithmetic and copies ran while one was open for 3% -> 3% of each run, Pallas kernels for 0% -> 0%
where the time goes in v1:
time: 577 us
  waiting for transfers between devices  336 us (58%)
  blocking collectives  117 us (20%)
  local copies, waits for them, and re-layouts  39 us (7%)
  matrix products  38.6 us (7%)
  starting transfers between devices  18.8 us (3%)
  between operations  14.3 us (2%)
  other arithmetic  11.4 us (2%)
    ppermute x6, waiting for transfers between devices, collected_by_bits(): other = lax.ppermute(pieces, axis, [(i, i ^ bit) for i in range(size)])  336 us
    all_gather x2, blocking collectives, merged(): gathered = jax.tree.map(lambda a: lax.all_gather(a, axis), part)  95.1 us
    all_to_all x1, blocking collectives, body(): lax.all_to_all(table, 'keys', split_axis=0, concat_axis=0, tiled=True)  22.2 us
    dot_general x1, matrix products, body(): jnp.einsum('re,tce->rtc', neighbours, lax.all_gather(kv_weight, 'keys', a...  18.7 us
    unnamed x16, local copies, waits for them, and re-layouts  16.6 us
    dot_general x1, matrix products, body(): jnp.einsum('chqk,ckhd->cqhd', weights, value_rows, preferred_element_type...  15.5 us
    ppermute x6, starting transfers between devices, collected_by_bits(): other = lax.ppermute(pieces, axis, [(i, i ^ bit) for i in range(size)])  12.5 us
    gather x1, local copies, waits for them, and re-layouts, body(): outgoing = neighbour_store[incoming]  11.9 us
  transfers between devices with their start and end apart: 8, of which 6 were waited for; matrix products, arithmetic and copies ran while one was open for 3% of the time, Pallas kernels for 0%

profile of v1, /device:TPU:1, one launch (start us, length us, event | category | flops | bytes accessed | tf_op | source)
XLA Modules:
  0.0 577.0 jit_solution(10456691162956033047)
XLA Ops:
  8.5 22.2 %all_to_all.17 = s32[64,1,2]{2,1,0:T(1,128)S(1)} all-to-all(s32[64,1,2]{2,1,0:T(1,128)S(1)} %bitcast.112), channel_id=1, replica_groups=mesh['keys'=64,'seq'=4] {'keys'}, dimensions={0} | all-to-all | bytes 1024 | tf_op jit(solution)/shard_map/all_to_all | solution.py:90
  31.1 11.9 %gather_fusion = bf16[128,64,896]{2,1,0:T(8,128)(2,1)} fusion(bf16[64,64,896]{2,1,0:T(8,128)(2,1)} %param.10, s32[1024]{0:T(1024)S(1)} %pad_clamp_fusion.1), kind=kCustom, calls=%fused_computation | custom fusion | bytes 29360640 | tf_op jit(solution)/shard_map/gather | solution.py:91
  43.0 6.2 %all-to-all-start.1 = ((bf16[64,2,64,896]{3,2,1,0:T(8,128)(2,1)}), bf16[64,2,64,896]{3,2,1,0:T(8,128)(2,1)}, u32[]{:S(2)}, u32[]{:S(2)}) async-start(bf16[64,2,64,896]{3,2,1,0:T(8,128)(2,1)} %bitcast.92), calls=%async_computation.1 | async-start | bytes 29360128 | tf_op jit(solution)/shard_map/all_to_all | solution.py:92
  52.1 315.1 %collective-permute-done.1 = bf16[2,6,768]{2,1,0:T(8,128)(2,1)S(1)} collective-permute-done((bf16[2,6,768]{2,1,0:T(8,128)(2,1)S(1)}, bf16[2,6,768]{2,1,0:T(8,128)(2,1)S(1)}, u32[]{:S(2)}, u32[]{:S(2)}) %collective-permute-start.1) | collective-permute-done | bytes 18464 | tf_op jit(solution)/shard_map/ppermute | solution.py:21
  367.3 4.3 collective-permute-done.2
  371.7 4.3 collective-permute-start.3
  376.0 4.6 collective-permute-done.3
  380.6 3.6 collective-permute-start.4
  384.3 4.4 collective-permute-done.4
  388.9 2.6 collective-permute-start.5
  391.7 1.6 copy.44
  393.3 6.6 %collective-permute-done.5 = bf16[32,6,768]{2,1,0:T(8,128)(2,1)S(1)} collective-permute-done((bf16[32,6,768]{2,1,0:T(8,128)(2,1)S(1)}, bf16[32,6,768]{2,1,0:T(8,128)(2,1)S(1)}, u32[]{:S(2)}, u32[]{:S(2)}) %collective-permute-start.5) | collective-permute-done | bytes 294944 | tf_op jit(solution)/shard_map/ppermute | solution.py:21
  400.8 5.0 top_k.8
  405.8 49.6 %all-gather = f32[24576,1]{0,1:T(1,128)S(1)} all-gather(f32[384,1]{0,1:T(1,128)S(1)} %get-tuple-element.161), channel_id=2, replica_groups=mesh['keys'=64,'seq'=4] {'keys'}, dimensions={0}, use_global_device_ids=true | all-gather | bytes 99840 | tf_op jit(solution)/shard_map/all_gather | solution.py:33
  455.4 45.5 %all-gather.1 = f32[24576,1]{0,1:T(1,128)S(1)} all-gather(f32[384,1]{0,1:T(1,128)S(1)} %get-tuple-element.160), channel_id=3, replica_groups=mesh['keys'=64,'seq'=4] {'keys'}, dimensions={0}, use_global_device_ids=true | all-gather | bytes 99840 | tf_op jit(solution)/shard_map/all_gather | solution.py:33
  503.3 4.3 while.17
  508.3 6.3 %gather_fusion.1 = bf16[24,64,896]{2,1,0:T(8,128)(2,1)S(1)} fusion(bf16[128,64,896]{2,1,0:T(8,128)(2,1)} %bitcast.23, s32[1024]{0:T(1024)S(1)} %pad_clamp_fusion), kind=kCustom, calls=%fused_computation.1 | custom fusion | bytes 5505120 | tf_op jit(solution)/shard_map/gather | solution.py:95
  514.6 18.7 %convolution_convert_fusion = bf16[1536,2,2048]{2,0,1:T(8,128)(2,1)} fusion(bf16[1536,896,1]{1,0,2:T(8,128)(2,1)S(1)} %bitcast.97, bf16[2,2048,896]{2,1,0:T(8,128)(2,1)} %all-gather.4.cloned.1.call-done), kind=kOutput, calls=%fused_computation.6 | convolution fusion | flops 11280580608 | bytes 22675456 | tf_op jit(solution)/shard_map/re,tce->rtc/dot_general | solution.py:97
  533.3 5.3 slice_bitcast_fusion.1
  538.6 2.3 copy.43
  541.0 3.7 fusion.5
  544.7 2.4 fusion.44
  547.1 5.0 copy.45
  552.1 15.5 %fusion.16 = bf16[6,64,16,128]{3,1,2,0:T(8,128)(2,1)S(1)} fusion(bf16[6,256,16,128]{3,2,1,0:T(8,128)(2,1)} %bitcast.94, f32[6,16,64]{2,1,0:T(8,128)S(1)} %fusion.44, f32[6,16,256,64]{2,3,1,0:T(8,128)} %copy-done.2), kind=kOutput, calls=%fused_computation.24 | convolution fusion | flops 411310336 | bytes 14180352 | tf_op jit(solution)/shard_map/chqk,ckhd->cqhd/dot_general | solution.py:112
  (189 shorter events, 14.2 us)
Async XLA Ops:
  7.2 393.3 %copy-start = (bf16[64,768]{1,0:T(8,128)(2,1)S(1)}, bf16[64,768]{1,0:T(8,128)(2,1)}, u32[]{:S(2)}) copy-start(bf16[64,768]{1,0:T(8,128)(2,1)} %param.9) | copy-start | bytes 294916
  43.0 6.3 %copy-start.4 = (bf16[6,768]{1,0:T(8,128)(2,1)S(1)}, bf16[6,768]{1,0:T(8,128)(2,1)}, u32[]{:S(2)}) copy-start(bf16[6,768]{1,0:T(8,128)(2,1)} %param.8) | copy-start | bytes 27652
  43.0 348.7 %copy-start.3 = (bf16[384,2048]{1,0:T(8,128)(2,1)S(1)}, bf16[384,2048]{1,0:T(8,128)(2,1)}, u32[]{:S(2)}) copy-start(bf16[384,2048]{1,0:T(8,128)(2,1)} %param.12) | copy-start | bytes 4718596
  43.0 465.3 %all-to-all-start.1 = ((bf16[64,2,64,896]{3,2,1,0:T(8,128)(2,1)}), bf16[64,2,64,896]{3,2,1,0:T(8,128)(2,1)}, u32[]{:S(2)}, u32[]{:S(2)}) async-start(bf16[64,2,64,896]{3,2,1,0:T(8,128)(2,1)} %bitcast.92), calls=%async_computation.1 | async-start | bytes 29360128 | tf_op jit(solution)/shard_map/all_to_all | solution.py:92
  49.2 465.3 %all-gather.4.cloned.1.call-start = ((), (), s32[]{:S(2)}) async-start(), calls=%async_computation.2 | async-start | bytes 7454720 | tf_op jit(solution)/shard_map/all_gather | solution.py:100
  49.3 1.6 collective-permute-start
  50.9 316.3 %collective-permute-start.1 = (bf16[2,6,768]{2,1,0:T(8,128)(2,1)S(1)}, bf16[2,6,768]{2,1,0:T(8,128)(2,1)S(1)}, u32[]{:S(2)}, u32[]{:S(2)}) collective-permute-start(bf16[2,6,768]{2,1,0:T(8,128)(2,1)S(1)} %get-tuple-element.163), channel_id=1, source_target_pairs={{0,8},{4,12},{8,0},{12,4},{16,24},{20,28},{24,16},{28,20},{32,40},... | collective-permute-start | bytes 55304 | tf_op jit(solution)/shard_map/ppermute | solution.py:21
  367.2 4.5 collective-permute-start.2
  371.7 8.9 %collective-permute-start.3 = (bf16[8,6,768]{2,1,0:T(8,128)(2,1)S(1)}, bf16[8,6,768]{2,1,0:T(8,128)(2,1)S(1)}, u32[]{:S(2)}, u32[]{:S(2)}) collective-permute-start(bf16[8,6,768]{2,1,0:T(8,128)(2,1)S(1)} %bitcast.104), channel_id=1, source_target_pairs={{0,32},{4,36},{8,40},{12,44},{16,48},{20,52},{24,56},{28,60},{32,0... | collective-permute-start | bytes 221192 | tf_op jit(solution)/shard_map/ppermute | solution.py:21
  380.6 8.1 %collective-permute-start.4 = (bf16[16,6,768]{2,1,0:T(8,128)(2,1)S(1)}, bf16[16,6,768]{2,1,0:T(8,128)(2,1)S(1)}, u32[]{:S(2)}, u32[]{:S(2)}) collective-permute-start(bf16[16,6,768]{2,1,0:T(8,128)(2,1)S(1)} %bitcast.102), channel_id=1, source_target_pairs={{0,64},{4,68},{8,72},{12,76},{16,80},{20,84},{24,88},{28,92},{32,9... | collective-permute-start | bytes 442376 | tf_op jit(solution)/shard_map/ppermute | solution.py:21
  388.9 11.0 %collective-permute-start.5 = (bf16[32,6,768]{2,1,0:T(8,128)(2,1)S(1)}, bf16[32,6,768]{2,1,0:T(8,128)(2,1)S(1)}, u32[]{:S(2)}, u32[]{:S(2)}) collective-permute-start(bf16[32,6,768]{2,1,0:T(8,128)(2,1)S(1)} %bitcast.100), channel_id=1, source_target_pairs={{0,128},{4,132},{8,136},{12,140},{16,144},{20,148},{24,152},{28,15... | collective-permute-start | bytes 884744 | tf_op jit(solution)/shard_map/ppermute | solution.py:21
  544.7 7.4 %copy-start.2 = (f32[6,16,256,64]{2,3,1,0:T(8,128)}, f32[6,16,256,64]{2,3,1,0:T(8,128)S(1)}, u32[]{:S(2)}) copy-start(f32[6,16,256,64]{2,3,1,0:T(8,128)S(1)} %fusion.5) | copy-start | bytes 18874372
  552.1 18.1 %copy-start.1 = (bf16[64,768]{1,0:T(8,128)(2,1)S(1)}, bf16[64,768]{1,0:T(8,128)(2,1)}, u32[]{:S(2)}) copy-start(bf16[64,768]{1,0:T(8,128)(2,1)} %param.9) | copy-start | bytes 294916
Sparse Core Ops, SparseCore 0:
  384.4 81.6 all-gather.3
